TPU v7x, 128 devices: a whole 4x4x4 slice. The times are simulated.
128 devices in a mesh: lat: 8 (over x, core), ord: 16 (over z, y).
Axes of the slice: x: 4, y: 4, z: 4, core: 2. Of those that a mesh axis runs over, the one named last changes fastest.
Arguments:
- residual: float32 [32, 3, 2, 64, 8192], P('ord', None, None, None, 'lat'), may hold values from -9 to 9
- direction: float32 [32, 3, 2, 64, 8192], P('ord', None, None, None, 'lat'), may hold values from -9 to 9
- legendre_zero: bfloat16 [32, 1024, 8192], P('ord', None, 'lat'), may hold values from -0.0625 to 0.0625
- legendre_plus: bfloat16 [32, 1024, 8192], P('ord', None, 'lat'), may hold values from -0.0625 to 0.0625
- legendre_minus: bfloat16 [32, 1024, 8192], P('ord', None, 'lat'), may hold values from -0.0625 to 0.0625
- order_pairs: int32 [32], replicated, may hold values from 0 to 8191, as said below
- hit_counts: int32 [1024, 16384], P(('lat', 'ord')), may hold values from 0 to 32768, as said below
- noise_weight: float32 [2], replicated, may hold values from 0.0003 to 0.0013
- prior_inverse: float32 [3, 8192], P(None, 'lat'), may hold values from 0.5 to 2
- prior_cross: float32 [8192], P('lat'), may hold values from -0.4 to 0.4
Outputs:
- residual_next: float32 [32, 3, 2, 64, 8192], P('ord', None, None, None, 'lat')
- direction_next: float32 [32, 3, 2, 64, 8192], P('ord', None, None, None, 'lat')
- step_size: float32 [64], replicated
Inputs may be any that keep to these rules, and one draw needn't show every extreme that they name: `order_pairs`: all entries are distinct; entries 2i and 2i+1 are m and 8191 - m with m < 4096; 0 and 8191 occur. `hit_counts`: 0 marks an unobserved pixel.
All inputs are finite; a program needn't handle non-finite values.
Results may differ from a plain program's by a relative error of at most 0.0043.
Values may be sent and summed in bfloat16 or wider, within the bound.
A program may use at most 192 MiB of HBM per device.

v0:
```python
import jax
import jax.numpy as jnp
from jax import lax
from jax.sharding import PartitionSpec as P


def cycle_table(order_values, parity, phase_count):
    phase_index = jnp.arange(phase_count, dtype=jnp.int32)
    orders = order_values[:, None]
    phase_units = (2 * orders * phase_index[None, :] + orders * parity) % (2 * phase_count)
    angles = jnp.pi * phase_units.astype(jnp.float32) / phase_count
    factor = jnp.where(order_values == 0, 1.0, 2.0).astype(jnp.float32)[:, None]
    phase_table = jnp.stack([factor * jnp.cos(angles), -factor * jnp.sin(angles)], 1)
    return phase_table.astype(jnp.bfloat16).reshape(2 * order_values.shape[0], phase_count)


def combine_forward_halves(intensity_field, positive_spin_field, negative_spin_field):
    leading_inphase = -positive_spin_field[..., 0, :] + negative_spin_field[..., 3, :]
    leading_quadrature = -positive_spin_field[..., 1, :] - negative_spin_field[..., 2, :]
    trailing_inphase = -positive_spin_field[..., 2, :] - negative_spin_field[..., 1, :]
    trailing_quadrature = -positive_spin_field[..., 3, :] + negative_spin_field[..., 0, :]
    return jnp.stack(
        [
            intensity_field,
            jnp.stack([leading_inphase, leading_quadrature], -2),
            jnp.stack([trailing_inphase, trailing_quadrature], -2),
        ],
        -3,
    )


def combine_transpose_halves(intensity_field, positive_spin_field, negative_spin_field):
    symmetric_inphase = -positive_spin_field[..., 0, 0, :, :] + negative_spin_field[..., 1, 1, :, :]
    symmetric_quadrature = (
        -positive_spin_field[..., 0, 1, :, :] - negative_spin_field[..., 1, 0, :, :]
    )
    bmode_inphase = -positive_spin_field[..., 1, 0, :, :] - negative_spin_field[..., 0, 1, :, :]
    bmode_quadrature = -positive_spin_field[..., 1, 1, :, :] + negative_spin_field[..., 0, 0, :, :]
    return jnp.stack(
        [
            intensity_field,
            jnp.stack([symmetric_inphase, symmetric_quadrature], -3),
            jnp.stack([bmode_inphase, bmode_quadrature], -3),
        ],
        -4,
    )


def prior_term(multipole_amplitudes, pivot_values_list, mixed_power_product):
    intensity_field = (
        pivot_values_list[0] * multipole_amplitudes[:, 0]
        + mixed_power_product * multipole_amplitudes[:, 1]
    )
    emode_field = (
        mixed_power_product * multipole_amplitudes[:, 0]
        + pivot_values_list[1] * multipole_amplitudes[:, 1]
    )
    bmode_field = pivot_values_list[2] * multipole_amplitudes[:, 2]
    return jnp.stack([intensity_field, emode_field, bmode_field], 1)


def pixel_pass(phases, cycle_base, order_values, hit_counts, component_weight):
    cycle_count = phases.shape[0]
    order_total = phases.shape[1]
    celestial_fields = phases.shape[4]
    phase_count = hit_counts.shape[1]
    even_table = cycle_table(order_values, 0, phase_count)
    odd_table = cycle_table(order_values, 1, phase_count)
    results = []
    for position in range(cycle_count):
        parity = (cycle_base + position) % 2
        phase_table = jnp.where(parity == 0, even_table, odd_table)
        flattened = (
            phases[position].transpose(1, 3, 0, 2).reshape(3 * celestial_fields, 2 * order_total)
        )
        sky_map = jnp.dot(flattened, phase_table, preferred_element_type=jnp.float32)
        weights = (
            hit_counts[position].astype(jnp.float32)[None, None, :]
            * component_weight[:, None, None]
        )
        weighted = (
            (sky_map.reshape(3, celestial_fields, phase_count) * weights)
            .astype(jnp.bfloat16)
            .reshape(3 * celestial_fields, phase_count)
        )
        adjoint = jnp.dot(weighted, phase_table.T, preferred_element_type=jnp.float32).astype(
            jnp.bfloat16
        )
        results.append(adjoint.reshape(3, celestial_fields, order_total, 2).transpose(2, 0, 3, 1))
    return jnp.stack(results, 0)


def per_device(
    residual,
    direction,
    legendre_zero,
    legendre_plus,
    legendre_minus,
    order_pairs,
    hit_counts,
    noise_weight,
    prior_inverse,
    prior_cross,
):
    longitude_wavenumbers = residual.shape[0]
    celestial_fields = residual.shape[3]
    degree_count = residual.shape[4]
    cycle_total = legendre_zero.shape[1]
    cycle_count = hit_counts.shape[0]
    phase_count = hit_counts.shape[1]
    lat_count = lax.axis_size("lat")
    ord_count = lax.axis_size("ord")
    lat_index = lax.axis_index("lat")
    ord_index = lax.axis_index("ord")
    sum_axes = (0, 1, 2, 4)
    local_orders = lax.dynamic_slice_in_dim(
        order_pairs, ord_index * longitude_wavenumbers, longitude_wavenumbers
    )
    degrees = lat_index * degree_count + jnp.arange(degree_count, dtype=jnp.int32)
    live_mask = (degrees[None, :] >= local_orders[:, None]).astype(jnp.float32)[
        :, None, None, None, :
    ]
    current = residual * live_mask
    search = direction * live_mask
    coefs_low = search.astype(jnp.bfloat16)
    norm_now = lax.psum(jnp.sum(current * current, axis=sum_axes), ("lat", "ord"))
    component_weight = jnp.stack([noise_weight[0], noise_weight[1], noise_weight[1]]) * (
        degree_count * lat_count / (cycle_total * phase_count)
    )
    cycle_base = (lat_index * ord_count + ord_index) * cycle_count
    temp_coefs = coefs_low[:, 0].reshape(longitude_wavenumbers, 2 * celestial_fields, degree_count)
    polar_coefs = coefs_low[:, 1:3].reshape(
        longitude_wavenumbers, 4 * celestial_fields, degree_count
    )
    zero_rows = legendre_zero
    plus_rows = legendre_plus
    minus_rows = legendre_minus
    intensity_field = jnp.einsum(
        "jrl,jxl->rjx", zero_rows, temp_coefs, preferred_element_type=jnp.float32
    )
    positive_spin_field = jnp.einsum(
        "jrl,jxl->rjx", plus_rows, polar_coefs, preferred_element_type=jnp.float32
    )
    negative_spin_field = jnp.einsum(
        "jrl,jxl->rjx", minus_rows, polar_coefs, preferred_element_type=jnp.float32
    )
    band_sum = lax.psum_scatter(
        combine_forward_halves(
            intensity_field.reshape(
                lax.axis_size("lat") * (cycle_total // lat_count),
                longitude_wavenumbers,
                2,
                celestial_fields,
            ),
            positive_spin_field.reshape(
                lax.axis_size("lat") * (cycle_total // lat_count),
                longitude_wavenumbers,
                4,
                celestial_fields,
            ),
            negative_spin_field.reshape(
                lax.axis_size("lat") * (cycle_total // lat_count),
                longitude_wavenumbers,
                4,
                celestial_fields,
            ),
        ),
        "lat",
        scatter_dimension=0,
        tiled=True,
    )
    adjoint = pixel_pass(
        lax.all_to_all(
            band_sum.astype(jnp.bfloat16), "ord", split_axis=0, concat_axis=1, tiled=True
        ),
        cycle_base,
        order_pairs,
        hit_counts,
        component_weight,
    )
    band_adjoint = lax.all_to_all(adjoint, "ord", split_axis=1, concat_axis=0, tiled=True)
    cycle_piece = lax.all_gather(band_adjoint, "lat", axis=0, tiled=True)
    associated_function_lines = cycle_piece.shape[0]
    zero_rows = legendre_zero
    plus_rows = legendre_plus
    minus_rows = legendre_minus
    temp_piece = cycle_piece[:, :, 0].reshape(
        associated_function_lines, longitude_wavenumbers, 2 * celestial_fields
    )
    polar_piece = cycle_piece[:, :, 1:3].reshape(
        associated_function_lines, longitude_wavenumbers, 4 * celestial_fields
    )
    temp_total = jnp.einsum(
        "jrl,rjx->jxl", zero_rows, temp_piece, preferred_element_type=jnp.float32
    )
    plus_total = jnp.einsum(
        "jrl,rjx->jxl", plus_rows, polar_piece, preferred_element_type=jnp.float32
    )
    minus_total = jnp.einsum(
        "jrl,rjx->jxl", minus_rows, polar_piece, preferred_element_type=jnp.float32
    )
    temp_total, plus_total, minus_total = (temp_total, plus_total, minus_total)
    data_term = combine_transpose_halves(
        temp_total.reshape(longitude_wavenumbers, 2, celestial_fields, degree_count),
        plus_total.reshape(longitude_wavenumbers, 2, 2, celestial_fields, degree_count),
        minus_total.reshape(longitude_wavenumbers, 2, 2, celestial_fields, degree_count),
    )
    image = live_mask * (data_term + prior_term(search, prior_inverse, prior_cross))
    curvature = lax.psum(jnp.sum(search * image, axis=sum_axes), ("lat", "ord"))
    step_size = norm_now / curvature
    residual_next = current - step_size[None, None, None, :, None] * image
    norm_next = lax.psum(jnp.sum(residual_next * residual_next, axis=sum_axes), ("lat", "ord"))
    norm_ratio = norm_next / norm_now
    direction_next = residual_next + norm_ratio[None, None, None, :, None] * search
    return (residual_next, direction_next, step_size)


def solution(mesh):
    in_specs = (
        P("ord", None, None, None, "lat"),
        P("ord", None, None, None, "lat"),
        P("ord", None, "lat"),
        P("ord", None, "lat"),
        P("ord", None, "lat"),
        P(),
        P(("lat", "ord"), None),
        P(),
        P(None, "lat"),
        P("lat"),
    )
    out_specs = (P("ord", None, None, None, "lat"), P("ord", None, None, None, "lat"), P())
    return jax.shard_map(
        per_device, mesh=mesh, in_specs=in_specs, out_specs=out_specs, check_vma=False
    )
```

profile of v0, /device:TPU:1, one launch (start us, length us, event | category | flops | bytes accessed | tf_op | source)
XLA Modules:
  0.0 549.7 jit_solution(7010693083663297459)
XLA Ops:
  8.0 2.8 fusion.47
  14.5 3.5 copy.187
  18.0 3.8 fusion.54
  23.2 3.5 copy.188
  26.7 3.5 copy.189
  30.2 3.5 copy.190
  33.7 3.5 copy.191
  37.3 3.5 copy.192
  40.8 3.5 copy.193
  44.3 3.5 copy.194
  47.8 4.9 fusion.52
  52.7 4.1 copy.148
  56.8 4.7 negate_subtract_fusion.1
  61.5 2.3 maximum_bitcast_fusion
  63.9 2.7 negate_add_fusion
  66.6 2.3 maximum_bitcast_fusion.1
  69.0 5.2 pad_maximum_fusion
  74.2 71.9 %all-reduce.3 = bf16[1024,2,3,2,64]{4,3,2,1,0:T(2,128)(2,1)} all-reduce(f32[1024,2,3,2,64]{4,3,2,1,0:T(2,128)} %pad_maximum_fusion), channel_id=2, replica_groups=mesh['lat'=8,'ord'=16] {'lat'}, use_global_device_ids=true, to_apply=%region_2.0.clone | all-reduce | flops 786432 | bytes 4718592
  149.5 7.8 %all-to-all-start = ((bf16[16,2,3072]{2,1,0:T(2,128)(2,1)}), bf16[16,2,3072]{2,1,0:T(2,128)(2,1)}, u32[]{:S(2)}, u32[]{:S(2)}) async-start(bf16[16,2,3072]{2,1,0:T(2,128)(2,1)} %reshape.955), calls=%async_computation | async-start | bytes 393216 | tf_op jit(solution)/shard_map/all_to_all | solution.py:173
  157.5 4.2 slice_convert_fusion
  163.7 17.0 %multiply_convert_fusion.3 = (bf16[32,1,16384]{2,0,1:T(8,128)(2,1)S(1)}, bf16[32,1,16384]{2,0,1:T(8,128)(2,1)S(1)}, bf16[32,1,16384]{2,0,1:T(8,128)(2,1)S(1)}, bf16[32,1,16384]{2,0,1:T(8,128)(2,1)S(1)}) fusion(s32[32]{0:T(128)S(1)} %broadcast_multiply_fusion.9, f32[32]{0:T(128)S(1)} %get-tuple-element.65, s32[32]{0:T(128)S(1)} %copy-done.43, ...), kind=kLoop, calls=%fused_computation.59 | loop fusion | flops 18874368 | bytes 4194816 | tf_op jit(solution)/shard_map/convert.2
  180.7 2.3 broadcast_select_fusion.1
  183.0 2.8 broadcast_select_fusion
  187.3 2.2 broadcast_select_fusion.2
  189.5 3.5 copy.157
  193.0 4.1 select_n.224
  197.1 5.1 copy.155
  202.2 4.3 select_n.220
  206.5 5.1 copy.153
  211.6 4.2 select_n.216
  215.7 5.1 copy.151
  220.8 4.1 select_n.212
  224.9 5.1 copy.159
  230.0 4.1 select_n.228
  234.1 5.1 copy.161
  239.1 4.1 select_n.232
  243.2 5.1 copy.163
  248.3 4.1 select_n.236
  252.4 5.1 copy.165
  257.5 4.5 select_n.240
  268.7 2.1 convolution_convert_fusion.4
  272.5 3.6 fusion.13
  276.1 2.1 convolution_convert_fusion.5
  279.9 3.6 fusion.14
  283.5 2.1 convolution_convert_fusion.6
  287.3 3.8 fusion.15
  296.4 3.6 fusion.11
  303.8 3.6 fusion.10
  311.2 3.6 fusion.9
  317.7 3.8 fusion.8
  321.6 2.7 convolution_convert_fusion
  333.6 14.0 %all_to_all.33 = bf16[16,2,3072]{2,1,0:T(2,128)(2,1)} all-to-all(bf16[16,2,3072]{2,1,0:T(2,128)(2,1)} %reshape.957), channel_id=1, replica_groups=mesh['lat'=8,'ord'=16] {'ord'}, dimensions={0} | all-to-all | bytes 393216 | tf_op jit(solution)/shard_map/all_to_all | solution.py:181
  352.7 23.8 %all-gather.2.cloned.1.call-done = bf16[1024,2,3,2,64]{4,0,3,2,1:T(8,128)(2,1)} async-done(((bf16[128,2,3,2,64]{4,0,3,2,1:T(8,128)(2,1)}), bf16[1024,2,3,2,64]{4,0,3,2,1:T(8,128)(2,1)}) %all-gather.2.cloned.1.call-update) | async-done | bytes 1572880 | tf_op jit(solution)/shard_map/all_gather | solution.py:182
  376.5 3.1 slice.204
  379.5 2.7 copy.169
  382.2 5.2 fusion.56
  387.4 2.6 fusion.57
  390.0 2.3 slice.203
  392.3 2.3 copy.168
  394.7 3.2 fusion.55
  403.7 65.3 %all-reduce.1 = (f32[64]{0:T(128)S(1)}, f32[64]{0:T(128)S(1)}) all-reduce(f32[64]{0:T(128)S(1)} %get-tuple-element.4, f32[64]{0:T(128)S(1)} %get-tuple-element.3), channel_id=1, replica_groups=mesh['lat'=8,'ord'=16] {'lat','ord'}, use_global_device_ids=true, to_apply=%region_1.0 | all-reduce | flops 128 | bytes 1024 | tf_op jit(solution)/shard_map/psum | solution.py:126
  469.0 5.8 %multiply_reduce_fusion = (f32[64]{0:T(128)S(1)}, f32[2,3,2,64,1024]{4,3,2,1,0:T(8,128)}) fusion(f32[2,1,2,64,1024]{4,3,2,1,0:T(8,128)} %get-tuple-element.25, f32[2,1,2,64,1024]{4,3,2,1,0:T(8,128)} %get-tuple-element.24, f32[2,1,2,64,1024]{4,3,2,1,0:T(8,128)} %get-tuple-element.23, f32[2,1,2,64,1024]{4,3,2,1,0:T(8,128)} %copy-done.8, ...), kind=kLoop, calls=%fused_computation.28 | loop fusion | flops 8650688 | bytes 12591616 | tf_op jit(solution)/shard_map/reduce_sum | solution.py:212
  474.8 63.2 %psum.23 = f32[64]{0:T(128)S(1)} all-reduce(f32[64]{0:T(128)S(1)} %get-tuple-element.7), channel_id=1, replica_groups=mesh['lat'=8,'ord'=16] {'lat','ord'}, use_global_device_ids=true, to_apply=%region_6.7 | all-reduce | flops 64 | bytes 512 | tf_op jit(solution)/shard_map/psum | solution.py:212
  538.0 4.7 multiply_add_fusion
  (155 shorter events, 59.8 us)
Async XLA Ops:
  8.0 3.8 copy-start.3
  10.9 2.2 copy-start.9
  61.4 2.4 copy-start.25
  61.5 2.4 copy-start.26
  61.5 2.4 copy-start.27
  61.5 2.4 copy-start.28
  66.6 2.4 copy-start.23
  74.2 71.9 %copy-start.45 = (u32[128]{0:T(128)S(1)}, u32[128]{0:T(128)}, u32[]{:S(2)}) copy-start(u32[128]{0:T(128)} %constant.114) | copy-start | bytes 1540
  74.2 83.3 %copy-start.43 = (s32[32]{0:T(128)S(1)}, s32[32]{0:T(128)}, u32[]{:S(2)}) copy-start(s32[32]{0:T(128)} %param.15) | copy-start | bytes 388
  146.1 15.6 %copy-start.44 = (f32[2]{0:T(128)S(1)}, f32[2]{0:T(128)}, u32[]{:S(2)}) copy-start(f32[2]{0:T(128)} %param.17) | copy-start | bytes 28
  149.5 112.4 %all-to-all-start = ((bf16[16,2,3072]{2,1,0:T(2,128)(2,1)}), bf16[16,2,3072]{2,1,0:T(2,128)(2,1)}, u32[]{:S(2)}, u32[]{:S(2)}) async-start(bf16[16,2,3072]{2,1,0:T(2,128)(2,1)} %reshape.955), calls=%async_computation | async-start | bytes 393216 | tf_op jit(solution)/shard_map/all_to_all | solution.py:173
  157.4 219.1 %all-gather.2.cloned.1.call-start = ((), (), s32[]{:S(2)}) async-start(), calls=%async_computation.2 | async-start | bytes 3538944 | tf_op jit(solution)/shard_map/all_gather | solution.py:182
  183.0 6.5 %copy-start = (bf16[32,2,16384]{2,0,1:T(8,128)(2,1)}, bf16[32,2,16384]{2,0,1:T(8,128)(2,1)S(1)}, u32[]{:S(2)}) copy-start(bf16[32,2,16384]{2,0,1:T(8,128)(2,1)S(1)} %get-tuple-element.19) | copy-start | bytes 6291460
  183.0 2.9 copy-start.29
  183.0 2.9 copy-start.30
  183.0 2.9 copy-start.31
  183.0 2.9 copy-start.32
  183.0 2.9 copy-start.33
  183.0 2.9 copy-start.34
  264.0 2.8 copy-start.1
  264.0 2.8 copy-start.24
  266.8 1.8 copy-start.22
  272.5 3.6 copy-start.21
  279.9 3.6 copy-start.20
  287.3 3.8 copy-start.19
  296.4 3.6 copy-start.18
  303.8 3.6 copy-start.17
  311.2 3.6 copy-start.16
  317.7 3.8 copy-start.15
  321.5 4.3 copy-start.37
  321.5 4.9 copy-start.36
  321.5 5.6 %copy-start.35 = (bf16[3,64,32,2]{1,0,3,2:T(4,128)(2,1)S(1)}, bf16[3,64,32,2]{1,0,3,2:T(4,128)(2,1)}, u32[]{:S(2)}) copy-start(bf16[3,64,32,2]{1,0,3,2:T(4,128)(2,1)} %reshape.926) | copy-start | bytes 73732
  321.5 6.2 %copy-start.38 = (bf16[3,64,32,2]{1,0,3,2:T(4,128)(2,1)S(1)}, bf16[3,64,32,2]{1,0,3,2:T(4,128)(2,1)}, u32[]{:S(2)}) copy-start(bf16[3,64,32,2]{1,0,3,2:T(4,128)(2,1)} %reshape.928) | copy-start | bytes 73732
  321.5 6.9 %copy-start.39 = (bf16[3,64,32,2]{1,0,3,2:T(4,128)(2,1)S(1)}, bf16[3,64,32,2]{1,0,3,2:T(4,128)(2,1)}, u32[]{:S(2)}) copy-start(bf16[3,64,32,2]{1,0,3,2:T(4,128)(2,1)} %reshape.930) | copy-start | bytes 73732
  321.5 7.5 %copy-start.40 = (bf16[3,64,32,2]{1,0,3,2:T(4,128)(2,1)S(1)}, bf16[3,64,32,2]{1,0,3,2:T(4,128)(2,1)}, u32[]{:S(2)}) copy-start(bf16[3,64,32,2]{1,0,3,2:T(4,128)(2,1)} %reshape.932) | copy-start | bytes 73732
  327.7 22.8 %copy-start.41 = (f32[1024]{0:T(1024)S(1)}, f32[1024]{0:T(1024)}, u32[]{:S(2)}) copy-start(f32[1024]{0:T(1024)} %param.19) | copy-start | bytes 12292
  382.2 5.2 copy-start.4
  382.2 5.2 copy-start.6
  394.7 3.2 copy-start.13
  394.7 3.6 copy-start.14
  397.9 1.1 copy-start.2
  398.3 1.2 copy-start.11
  398.3 1.6 copy-start.12
  398.8 2.9 copy-start.5
  398.8 3.2 copy-start.10
  398.9 4.8 copy-start.7
  399.0 4.7 copy-start.8
  469.0 5.8 %copy-start.42 = (f32[64]{0:T(128)}, f32[64]{0:T(128)S(1)}, u32[]{:S(2)}) copy-start(f32[64]{0:T(128)S(1)} %div.17) | copy-start | bytes 772
Sparse Core Ops, SparseCore 0:
  349.8 26.5 all-gather.1
where the time goes:
time: 556 us; the launch traced here: 550 us
  blocking collectives  214 us (38%)
  local copies, waits for them, and re-layouts  156 us (28%)
  other arithmetic  66.4 us (12%)
  matrix products  65.8 us (12%)
  waiting for transfers between devices  23.8 us (4%)
  between operations  15.7 us (3%)
  starting transfers between devices  7.85 us (1%)
    select_n x16, local copies, waits for them, and re-layouts, pixel_pass(): phase_table = jnp.where(parity == 0, even_table, odd_table)  72.4 us
    unnamed x1, blocking collectives  71.9 us
    psum x1, blocking collectives, per_device(): lax.psum(jnp.sum(current * current, axis=sum_axes), ('lat', 'ord'))  65.3 us
    psum x1, blocking collectives, per_device(): lax.psum(jnp.sum(residual_next * residual_next, axis=sum_axes), ('lat', '...  63.2 us
    unnamed x112, local copies, waits for them, and re-layouts  42.6 us
    dot_general x8, matrix products, pixel_pass(): jnp.dot(flattened, phase_table, preferred_element_type=jnp.float32)  27.2 us
    all_gather x1, waiting for transfers between devices, per_device(): cycle_piece = lax.all_gather(band_adjoint, 'lat', axis=0, tiled=True)  23.8 us
    dot_general x8, matrix products, pixel_pass(): jnp.dot(weighted, phase_table.T, preferred_element_type=jnp.float32)  17.6 us
  transfers between devices with their start and end apart: 2, of which 1 were waited for; matrix products, arithmetic and copies ran while one was open for 20% of the time, Pallas kernels for 0%

commit v1 on v0

v1 whole, which is shorter than its diff:
```python
import functools
import math

import jax
import jax.numpy as jnp
from jax import lax
from jax.experimental import pallas as pl
from jax.experimental.pallas import tpu as pltpu
from jax.sharding import PartitionSpec as P

MESH = pl.DeviceIdType.MESH
BF = jnp.bfloat16
F32 = jnp.float32
NT = (((1,), (1,)), ((), ()))

LAT = 8
ORD = 16
KM = 64
CIRC = 8
NPHI = 16384
LMAX = 8192
LINES = 1024
DEG = LMAX // LAT
CHUNKS = ((0, 1), (1, 2))
SCALE = LMAX / (LINES * NPHI)


def weight_kernel(orders, hits, g, z, w, rz, rw, lhs, rhs, acc):
    m_total = orders.shape[0]
    half = NPHI // 2
    lane = lax.broadcasted_iota(jnp.int32, (8, 128), 1)
    parity = lax.broadcasted_iota(jnp.int32, (8, 128), 0) & 1

    def seed(m, carry):
        order = orders[m]
        units = (2 * order * lane + order * parity) & (2 * NPHI - 1)
        angle = units.astype(F32) * (math.pi / NPHI)
        size = jnp.where(order == 0, 1.0, 2.0).astype(F32)
        re = size * jnp.cos(angle)
        im = -size * jnp.sin(angle)
        turn = jnp.full((8, 128), (256 * order) & (2 * NPHI - 1), jnp.int32)
        turn = turn.astype(F32) * (math.pi / NPHI)
        wre = jnp.cos(turn)
        wim = -jnp.sin(turn)
        sign = jnp.full((8, 128), 1 - 2 * (order & 1), jnp.int32).astype(F32)
        z[m, 0] = re
        z[m, 1] = im
        w[m, 0] = wre
        w[m, 1] = wim
        w[m, 2] = sign
        for par in range(2):
            rz[par, 0, pl.ds(m, 1), :] = re[par : par + 1]
            rz[par, 1, pl.ds(m, 1), :] = im[par : par + 1]
        rw[0, pl.ds(m, 1), :] = wre[:1]
        rw[1, pl.ds(m, 1), :] = wim[:1]
        rw[2, pl.ds(m, 1), :] = sign[:1]
        return carry

    lax.fori_loop(0, m_total, seed, 0)
    acc[...] = jnp.zeros_like(acc)

    def step(n, carry):
        base = pl.multiple_of(n * 512, 512)
        first = [hits[:, pl.ds(base + a * 128, 128)].astype(F32) for a in range(4)]
        second = [hits[:, pl.ds(half + base + a * 128, 128)].astype(F32) for a in range(4)]

        def pair(mm, inner):
            out = [[[], []] for _ in range(4)]
            out2 = [[[], []] for _ in range(4)]
            for q in range(2):
                m = 2 * mm + q
                re, im = z[m, 0], z[m, 1]
                wre, wim, sign = w[m, 0], w[m, 1], w[m, 2]
                for a in range(4):
                    flipped = second[a] * sign
                    out[a][0].append(re * first[a])
                    out[a][1].append(im * first[a])
                    out2[a][0].append(re * flipped)
                    out2[a][1].append(im * flipped)
                    re, im = re * wre - im * wim, re * wim + im * wre
                z[m, 0] = re
                z[m, 1] = im
            rows = pl.ds(pl.multiple_of(mm * 16, 16), 16)
            for a in range(4):
                for s in range(2):
                    lhs[s, rows, a * 128 : (a + 1) * 128] = jnp.concatenate(out[a][s], 0).astype(BF)
                    lhs[s, rows, 512 + a * 128 : 512 + (a + 1) * 128] = jnp.concatenate(
                        out2[a][s], 0
                    ).astype(BF)
            return inner

        lax.fori_loop(0, m_total // 2, pair, 0)
        wre, wim, sign = rw[0], rw[1], rw[2]
        for par in range(2):
            re, im = rz[par, 0], rz[par, 1]
            for a in range(4):
                for s, value in ((0, re), (1, im)):
                    rows = slice(par * 64 + s * 32, par * 64 + s * 32 + 32)
                    rhs[rows, a * 128 : (a + 1) * 128] = value.astype(BF)
                    rhs[rows, 512 + a * 128 : 512 + (a + 1) * 128] = (value * sign).astype(BF)
                re, im = re * wre - im * wim, re * wim + im * wre
            rz[par, 0] = re
            rz[par, 1] = im
        for s in range(2):
            acc[s] += lax.dot_general(lhs[s], rhs[...], NT, preferred_element_type=F32)
        return carry

    lax.fori_loop(0, half // 512, step, 0)

    row = lax.broadcasted_iota(jnp.int32, (256, 128), 0)
    lane_from = lax.broadcasted_iota(jnp.int32, (128, 256), 0)
    lane_to = lax.broadcasted_iota(jnp.int32, (128, 256), 1)
    keep = (lax.broadcasted_iota(jnp.int32, (256, 256), 0) & 7) == (
        lax.broadcasted_iota(jnp.int32, (256, 256), 1) & 7
    )
    for s in range(2):
        total = acc[s]
        total = jnp.where((row & 1) == 0, total, pltpu.roll(total, 64, 1)).astype(BF)
        for u in range(2):
            other = s if u == 0 else 1 - s
            spread = jnp.where(lane_from == other * 32 + lane_to // 8, 1.0, 0.0).astype(BF)
            block = jnp.dot(total, spread, preferred_element_type=F32)
            g[s * 256 : (s + 1) * 256, u * 256 : (u + 1) * 256] = jnp.where(
                keep, block, 0.0
            ).astype(BF)


def circle_weights(orders, hits):
    return pl.pallas_call(
        weight_kernel,
        out_shape=jax.ShapeDtypeStruct((512, 512), BF),
        in_specs=[
            pl.BlockSpec(memory_space=pltpu.SMEM),
            pl.BlockSpec(memory_space=pltpu.VMEM),
        ],
        out_specs=pl.BlockSpec(memory_space=pltpu.VMEM),
        scratch_shapes=[
            pltpu.VMEM((32, 2, 8, 128), F32),
            pltpu.VMEM((32, 3, 8, 128), F32),
            pltpu.VMEM((2, 2, 32, 128), F32),
            pltpu.VMEM((3, 32, 128), F32),
            pltpu.VMEM((2, 256, 1024), BF),
            pltpu.VMEM((128, 1024), BF),
            pltpu.VMEM((2, 256, 128), F32),
        ],
        compiler_params=pltpu.CompilerParams(vmem_limit_bytes=16 * 2**20),
    )(orders, hits)


def step_kernel(
    orders, noise, prior, cross, g, residual, direction, lz, lp, lm,
    image_out, scal_out,
    res_v, dir_v, lz_v, lp_v, lm_v, ct, cx, cy,
    part, prec, summed, relay, fin, phases, rbuf, adj, zbuf, wbuf, img, stat, st1, st2,
    load_sem, out_sem, pair_s, pair_r, ring_s, ring_r, a2a_s, a2a_r, ag_s, ag_r, red_s, red_r,
):
    lat = lax.axis_index("lat")
    ord_ = lax.axis_index("ord")
    x = lat // 2
    core = lat % 2
    partner = 2 * x + (1 - core)
    right = 2 * ((x + 1) % 4) + core
    left = 2 * ((x + 3) % 4) + core
    sent = []

    def remote(src, dst, ssem, rsem, **where):
        copy = pltpu.make_async_remote_copy(
            src_ref=src, dst_ref=dst, send_sem=ssem, recv_sem=rsem,
            device_id=where, device_id_type=MESH,
        )
        copy.start()
        sent.append(copy)
        return copy

    loads = {}

    def load(name, src, dst, i):
        copy = pltpu.make_async_copy(src, dst, load_sem.at[i])
        copy.start()
        loads[name] = copy

    load("dir", direction, dir_v, 0)
    for i, d in enumerate((2, 1, 3, 0)):
        rows = pl.ds(pl.multiple_of(((x + d) % 4) * 256, 256), 256)
        load(("z", d), lz.at[:, rows, :], lz_v.at[:, d], 1 + i)
    for i, d in enumerate((2, 1, 3, 0)):
        rows = pl.ds(pl.multiple_of(((x + d) % 4) * 256, 256), 256)
        load(("p", d), lp.at[:, rows, :], lp_v.at[:, d], 5 + i)
        load(("m", d), lm.at[:, rows, :], lm_v.at[:, d], 9 + i)
    load("res", residual, res_v, 13)

    barrier = pltpu.get_barrier_semaphore()

    def greet_lat(off, carry):
        pl.semaphore_signal(
            barrier, inc=1, device_id={"lat": (lat + off) % LAT}, device_id_type=MESH
        )
        return carry

    def greet_ord(off, carry):
        pl.semaphore_signal(
            barrier, inc=1, device_id={"ord": (ord_ + off) % ORD}, device_id_type=MESH
        )
        return carry

    lax.fori_loop(1, LAT, greet_lat, 0)
    lax.fori_loop(1, ORD, greet_ord, 0)

    degree = lax.broadcasted_iota(jnp.int32, (8, DEG), 1) + lat * DEG
    live = [jnp.where(degree >= orders[2 * ord_ + o], 1.0, 0.0).astype(F32) for o in range(2)]
    loads["dir"].wait()
    for o in range(2):
        mask = jnp.broadcast_to(live[o][:1], (KM, DEG))
        for s in range(2):
            rows = slice(s * KM, (s + 1) * KM)
            ct[o, rows, :] = (dir_v[o, 0, rows, :] * mask).astype(BF)
            e = (dir_v[o, 1, rows, :] * mask).astype(BF)
            b = (dir_v[o, 2, rows, :] * mask).astype(BF)
            cx[o, s * 64 : s * 64 + 64, :] = -e
            cx[o, 128 + s * 64 : 192 + s * 64, :] = -b
            if s == 0:
                cy[o, 192:256, :] = e
                cy[o, 64:128, :] = -b
            else:
                cy[o, 128:192, :] = -e
                cy[o, 0:64, :] = b

    pl.semaphore_wait(barrier, LAT + ORD - 2)

    def groups(first, second):
        both = jnp.concatenate([first.reshape(32, 8, 128), second.reshape(32, 8, 128)], 1)
        return both.astype(BF).reshape(2, 16, 16, 128)

    pairs = {}

    def synth(ch, d):
        lo, count = CHUNKS[ch]
        if ch == 0:
            loads["z", d].wait()
            got = [
                lax.dot_general(lz_v[o, d], ct[o], NT, preferred_element_type=F32) for o in range(2)
            ]
            part[d, :, 0] = groups(got[0], got[1])
        else:
            loads["p", d].wait()
            loads["m", d].wait()
            got = [
                lax.dot_general(lp_v[o, d], cx[o], NT, preferred_element_type=F32)
                + lax.dot_general(lm_v[o, d], cy[o], NT, preferred_element_type=F32)
                for o in range(2)
            ]
            part[d, :, 1] = groups(got[0][:, :128], got[1][:, :128])
            part[d, :, 2] = groups(got[0][:, 128:], got[1][:, 128:])
        cs = pl.ds(lo, count)
        pairs[ch, d] = remote(
            part.at[d, 1 - core, cs], prec.at[d, cs], pair_s.at[ch, d], pair_r.at[ch, d], lat=partner
        )

    rings = {}

    def chunk(ch):
        lo, count = CHUNKS[ch]
        return lo, count, pl.ds(lo, count), slice(lo, lo + count)

    def pair_sum(ch, d, lo_g, hi_g):
        _, _, _, c = chunk(ch)
        return part[d, core, c, lo_g:hi_g].astype(F32) + prec[d, c, lo_g:hi_g].astype(F32)

    def ring_far(ch):
        _, _, cs, c = chunk(ch)
        pairs[ch, 2].wait_recv()
        summed[2, c] = pair_sum(ch, 2, 0, 16).astype(BF)
        a, b = pl.ds(0, 8), pl.ds(8, 8)
        rings[ch, 0] = remote(
            summed.at[2, cs, a], relay.at[0, cs], ring_s.at[ch, 0], ring_r.at[ch, 0], lat=right
        )
        rings[ch, 1] = remote(
            summed.at[2, cs, b], relay.at[1, cs], ring_s.at[ch, 1], ring_r.at[ch, 1], lat=left
        )

    def ring_near(ch, d, part_no):
        _, _, cs, c = chunk(ch)
        side = 0 if d == 1 else 1
        if part_no == 0:
            pairs[ch, d].wait_recv()
            lo_g = 8 if d == 1 else 0
            summed[d, c, lo_g : lo_g + 8] = pair_sum(ch, d, lo_g, lo_g + 8).astype(BF)
        else:
            lo_g = 0 if d == 1 else 8
            rings[ch, side].wait_recv()
            summed[d, c, lo_g : lo_g + 8] = (
                pair_sum(ch, d, lo_g, lo_g + 8) + relay[side, c].astype(F32)
            ).astype(BF)
        sem = 2 + side * 2 + part_no
        span = pl.ds(lo_g, 8)
        rings[ch, sem] = remote(
            summed.at[d, cs, span], fin.at[side, cs, span], ring_s.at[ch, sem], ring_r.at[ch, sem],
            lat=right if d == 1 else left,
        )

    def ring_end(ch):
        _, _, _, c = chunk(ch)
        pairs[ch, 0].wait_recv()
        for sem in (2, 4, 3, 5):
            rings[ch, sem].wait_recv()
        phases[c] = (
            pair_sum(ch, 0, 0, 16) + fin[0, c].astype(F32) + fin[1, c].astype(F32)
        ).astype(BF)

    def exchange(ch, way, src, dst):
        lo, count, cs, c = chunk(ch)

        def copy(off):
            to = (ord_ + off) % ORD
            return pltpu.make_async_remote_copy(
                src_ref=src.at[cs, to], dst_ref=dst.at[cs, ord_],
                send_sem=a2a_s.at[way, ch, off], recv_sem=a2a_r.at[way, ch, off],
                device_id={"ord": to}, device_id_type=MESH,
            )

        def go(off, carry):
            copy(off).start()
            return carry

        def wait(off, carry):
            copy(off).wait_recv()
            return carry

        def drain(off, carry):
            copy(off).wait_send()
            return carry

        lax.fori_loop(1, ORD, go, 0)
        for i in range(lo, lo + count):
            dst[i, ord_] = src[i, ord_]
        return (
            lambda: lax.fori_loop(1, ORD, wait, 0),
            lambda: lax.fori_loop(1, ORD, drain, 0),
        )

    left_half = lax.broadcasted_iota(jnp.int32, (256, 128), 1) < KM

    def apply(ch):
        lo, count, _, _ = chunk(ch)
        for i in range(lo, lo + count):
            here = rbuf[i].reshape(256, 128)
            swapped = pltpu.roll(here.astype(F32), KM, 1).astype(BF)
            out = jnp.dot(
                g[...], jnp.concatenate([here, swapped], 0), preferred_element_type=F32
            )
            out = jnp.where(left_half, out[:256], out[256:]) * (noise[min(i, 1)] * SCALE)
            adj[i] = out.astype(BF).reshape(16, 16, 128)

    def turn(ch):
        lo, count, _, _ = chunk(ch)
        for i in range(lo, lo + count):
            got = zbuf[i].astype(F32).reshape(16, 2, 8, 128)
            for o in range(2):
                wbuf[lat, i, o] = got[:, o].reshape(128, 128).T.astype(BF)

    gathers = {}

    def gather(ch, i, slot, cs, o, **where):
        view = wbuf.at[slot, cs] if o is None else wbuf.at[slot, cs, o]
        gathers[ch, i] = remote(view, view, ag_s.at[ch, i], ag_r.at[ch, i], **where)

    def gather_start(ch):
        _, _, cs, _ = chunk(ch)
        gather(ch, 1, lat, cs, None, lat=right)
        gather(ch, 2, lat, cs, None, lat=left)
        gather(ch, 0, lat, cs, None, lat=partner)

    def gather_near(ch):
        _, _, cs, _ = chunk(ch)
        gathers[ch, 1].wait_recv()
        gather(ch, 3, left, cs, 0, lat=right)
        gather(ch, 5, left, cs, None, lat=partner)
        gathers[ch, 2].wait_recv()
        gather(ch, 4, right, cs, 1, lat=left)
        gather(ch, 6, right, cs, None, lat=partner)

    def gather_far(ch):
        _, _, cs, _ = chunk(ch)
        far = 2 * ((x + 2) % 4) + core
        gathers[ch, 3].wait_recv()
        gather(ch, 7, far, cs, 0, lat=partner)
        gathers[ch, 4].wait_recv()
        gather(ch, 8, far, cs, 1, lat=partner)

    gather_waits = {0: (0,), 3: (5,), 1: (6,), 2: (7, 8)}

    def analysis(ch, d, first):
        slot = 2 * ((x + d) % 4)
        for i in gather_waits[d]:
            gathers[ch, i].wait_recv()
        for o in range(2):
            if ch == 0:
                lhs = jnp.concatenate([wbuf[slot, 0, o], wbuf[slot + 1, 0, o]], 1)
                got = jnp.dot(lhs, lz_v[o, d], preferred_element_type=F32)
                img[o, 0] = got if first else img[o, 0] + got
            else:
                q = jnp.concatenate([wbuf[slot, 1, o], wbuf[slot + 1, 1, o]], 1)
                u = jnp.concatenate([wbuf[slot, 2, o], wbuf[slot + 1, 2, o]], 1)
                straight = jnp.concatenate([-q, -u], 0)
                crossed = jnp.concatenate([u[64:], -u[:64], -q[64:], q[:64]], 0)
                got = jnp.dot(straight, lp_v[o, d], preferred_element_type=F32) + jnp.dot(
                    crossed, lm_v[o, d], preferred_element_type=F32
                )
                for c in range(2):
                    piece = got[c * 128 : (c + 1) * 128]
                    img[o, 1 + c] = piece if first else img[o, 1 + c] + piece

    synth(0, 2)
    synth(0, 1)
    ring_far(0)
    synth(0, 3)
    ring_near(0, 1, 0)
    synth(0, 0)
    ring_near(0, 3, 0)
    ring_near(0, 1, 1)
    ring_near(0, 3, 1)
    synth(1, 2)
    synth(1, 1)
    ring_far(1)
    synth(1, 3)
    ring_near(1, 1, 0)
    synth(1, 0)
    ring_near(1, 3, 0)
    ring_end(0)
    wait_a, drain_a = exchange(0, 0, phases, rbuf)
    ring_near(1, 1, 1)
    ring_near(1, 3, 1)
    wait_a()
    apply(0)
    wait_b, drain_b = exchange(0, 1, adj, zbuf)
    ring_end(1)
    wait_c, drain_c = exchange(1, 0, phases, rbuf)
    wait_b()
    turn(0)
    gather_start(0)
    wait_c()
    apply(1)
    wait_d, drain_d = exchange(1, 1, adj, zbuf)
    gather_near(0)
    analysis(0, 0, True)
    wait_d()
    turn(1)
    gather_start(1)
    gather_far(0)
    analysis(0, 3, False)
    analysis(0, 1, False)
    analysis(0, 2, False)
    analysis(1, 0, True)
    gather_near(1)
    analysis(1, 3, False)
    analysis(1, 1, False)
    gather_far(1)
    analysis(1, 2, False)
    loads["res"].wait()

    column = lax.broadcasted_iota(jnp.int32, (8, 128), 1)
    stat[...] = jnp.zeros_like(stat)

    def finish(i, carry):
        k0 = pl.multiple_of(i * 8, 8)
        sums = [jnp.zeros((8, DEG), F32) for _ in range(4)]
        for o in range(2):
            for s in range(2):
                rows = pl.ds(s * KM + k0, 8)
                search = [dir_v[o, c, rows, :] * live[o] for c in range(3)]
                priors = (
                    prior[0:1] * search[0] + cross[...] * search[1],
                    cross[...] * search[0] + prior[1:2] * search[1],
                    prior[2:3] * search[2],
                )
                for c in range(3):
                    image = live[o] * (img[o, c, rows, :] + priors[c])
                    img[o, c, rows, :] = image
                    current = res_v[o, c, rows, :] * live[o]
                    sums[0] += current * current
                    sums[1] += search[c] * image
                    sums[2] += current * image
                    sums[3] += image * image
        tile = jnp.zeros((8, 128), F32)
        for q in range(4):
            tile = jnp.where(column == q, jnp.sum(sums[q], axis=1, keepdims=True), tile)
        stat[pl.ds(k0, 8), :] = tile
        return carry

    lax.fori_loop(0, KM // 8, finish, 0)
    store = pltpu.make_async_copy(img, image_out, out_sem)
    store.start()

    def all_reduce(buf, axis, size, me, stage):
        def copy(off):
            return pltpu.make_async_remote_copy(
                src_ref=buf.at[me], dst_ref=buf.at[me],
                send_sem=red_s.at[stage, off], recv_sem=red_r.at[stage, off],
                device_id={axis: (me + off) % size}, device_id_type=MESH,
            )

        def go(off, carry):
            copy(off).start()
            return carry

        def wait(off, carry):
            copy(off).wait()
            return carry

        lax.fori_loop(1, size, go, 0)
        lax.fori_loop(1, size, wait, 0)
        total = buf[0]
        for i in range(1, size):
            total = total + buf[i]
        return total

    st1[lat] = stat[...].T[:8]
    st2[ord_] = all_reduce(st1, "lat", LAT, lat, 0)
    total = all_reduce(st2, "ord", ORD, ord_, 1)
    norm_now, curvature, mixed, square = (total[q : q + 1] for q in range(4))
    step_size = norm_now / curvature
    norm_next = norm_now + step_size * (step_size * square - 2.0 * mixed)
    ratio = norm_next / norm_now
    sub = lax.broadcasted_iota(jnp.int32, (8, 128), 0)
    scal_out[...] = jnp.where(sub == 0, step_size, ratio)

    for drain in (drain_a, drain_b, drain_c, drain_d):
        drain()
    for copy in sent:
        copy.wait_send()
    store.wait()


def cg_sums(orders, noise, prior, cross, g, residual, direction, lz, lp, lm):
    smem = pl.BlockSpec(memory_space=pltpu.SMEM)
    vmem = pl.BlockSpec(memory_space=pltpu.VMEM)
    hbm = pl.BlockSpec(memory_space=pl.ANY)
    dma = pltpu.SemaphoreType.DMA
    nch = len(CHUNKS)
    return pl.pallas_call(
        step_kernel,
        out_shape=(
            jax.ShapeDtypeStruct((2, 3, 128, DEG), F32),
            jax.ShapeDtypeStruct((8, 128), F32),
        ),
        in_specs=[smem, smem, vmem, vmem, vmem, hbm, hbm, hbm, hbm, hbm],
        out_specs=(hbm, vmem),
        scratch_shapes=[
            pltpu.VMEM((2, 3, 128, DEG), F32),
            pltpu.VMEM((2, 3, 128, DEG), F32),
            pltpu.VMEM((2, 4, 256, DEG), BF),
            pltpu.VMEM((2, 4, 256, DEG), BF),
            pltpu.VMEM((2, 4, 256, DEG), BF),
            pltpu.VMEM((2, 128, DEG), BF),
            pltpu.VMEM((2, 256, DEG), BF),
            pltpu.VMEM((2, 256, DEG), BF),
            pltpu.VMEM((4, 2, 3, 16, 16, 128), BF),
            pltpu.VMEM((4, 3, 16, 16, 128), BF),
            pltpu.VMEM((4, 3, 16, 16, 128), BF),
            pltpu.VMEM((2, 3, 8, 16, 128), BF),
            pltpu.VMEM((2, 3, 16, 16, 128), BF),
            pltpu.VMEM((3, 16, 16, 128), BF),
            pltpu.VMEM((3, 16, 16, 128), BF),
            pltpu.VMEM((3, 16, 16, 128), BF),
            pltpu.VMEM((3, 16, 16, 128), BF),
            pltpu.VMEM((LAT, 3, 2, 128, 128), BF),
            pltpu.VMEM((2, 3, 128, DEG), F32),
            pltpu.VMEM((128, 128), F32),
            pltpu.VMEM((LAT, 8, 128), F32),
            pltpu.VMEM((ORD, 8, 128), F32),
            dma((14,)),
            dma,
            dma((nch, 4)),
            dma((nch, 4)),
            dma((nch, 6)),
            dma((nch, 6)),
            dma((2, nch, ORD)),
            dma((2, nch, ORD)),
            dma((nch, 9)),
            dma((nch, 9)),
            dma((2, ORD)),
            dma((2, ORD)),
        ],
        compiler_params=pltpu.CompilerParams(
            collective_id=0, has_side_effects=True, vmem_limit_bytes=44 * 2**20
        ),
    )(orders, noise, prior, cross, g, residual, direction, lz, lp, lm)


def per_device(
    residual,
    direction,
    legendre_zero,
    legendre_plus,
    legendre_minus,
    order_pairs,
    hit_counts,
    noise_weight,
    prior_inverse,
    prior_cross,
):
    shape = residual.shape
    flat = (2, 3, 128, DEG)
    g = circle_weights(order_pairs, hit_counts)
    image, scalars = cg_sums(
        order_pairs,
        noise_weight,
        prior_inverse,
        prior_cross.reshape(1, DEG),
        g,
        residual.reshape(flat),
        direction.reshape(flat),
        legendre_zero,
        legendre_plus,
        legendre_minus,
    )
    step_size = scalars[0, :KM]
    ratio = scalars[1, :KM]
    mine = lax.dynamic_slice_in_dim(order_pairs, lax.axis_index("ord") * 2, 2)
    degrees = lax.axis_index("lat") * DEG + jnp.arange(DEG, dtype=jnp.int32)
    live = (degrees[None, :] >= mine[:, None]).astype(F32)[:, None, None, None, :]
    residual_next = (
        residual * live - step_size[None, None, None, :, None] * image.reshape(shape)
    )
    direction_next = residual_next + ratio[None, None, None, :, None] * (direction * live)
    return residual_next, direction_next, step_size


def solution(mesh):
    coef = P("ord", None, None, None, "lat")
    table = P("ord", None, "lat")
    in_specs = (
        coef, coef, table, table, table, P(), P(("lat", "ord"), None), P(), P(None, "lat"), P("lat"),
    )
    return jax.shard_map(
        per_device, mesh=mesh, in_specs=in_specs, out_specs=(coef, coef, P()), check_vma=False
    )
```

time: 556 us -> 88.4 us (0.16); the launches traced: 550 us -> 88 us
  blocking collectives: 214 us -> 0 us
  local copies, waits for them, and re-layouts: 156 us -> 8.93 us
  Pallas kernels: 0 us -> 74.3 us
  matrix products: 65.8 us -> 0 us
  other arithmetic: 66.4 us -> 4.08 us
  waiting for transfers between devices: 23.8 us -> 0 us
  between operations: 15.7 us -> 0.68 us
  starting transfers between devices: 7.85 us -> 0 us
    psum x2 -> x0, blocking collectives: 128 us -> none  [the longest x1 65.3 us: per_device(): lax.psum(jnp.sum(current * current, axis=sum_axes), ('lat', 'ord'))]
    pallas_call x0 -> x2, Pallas kernels: none -> 74.3 us  [the longest x1 58.5 us: cg_sums(): pl.pallas_call(step_kernel, out_shape=(jax.ShapeDtypeStruct((2, 3, 128, D...]
    select_n x16 -> x0, local copies, waits for them, and re-layouts: 72.4 us -> none  [pixel_pass(): phase_table = jnp.where(parity == 0, even_table, odd_table)]
    unnamed x1 -> x0, blocking collectives: 71.9 us -> none
    dot_general x22 -> x0, matrix products: 65.8 us -> none  [the longest x8 27.2 us: pixel_pass(): jnp.dot(flattened, phase_table, preferred_element_type=jnp.float32)]
    unnamed x112 -> x18, local copies, waits for them, and re-layouts: 42.6 us -> 8.19 us
    another operation x6 -> x0, other arithmetic: 27.1 us -> none
    all_gather x1 -> x0, waiting for transfers between devices: 23.8 us -> none  [per_device(): cycle_piece = lax.all_gather(band_adjoint, 'lat', axis=0, tiled=True)]
  transfers between devices with their start and end apart: 2 -> 0, of which waited for: 1 -> 0; matrix products, arithmetic and copies ran while one was open for 20% -> 0% of each run, Pallas kernels for 0% -> 0%
where the time goes in v1:
time: 88.4 us; the launch traced here: 88 us
  Pallas kernels  74.3 us (84%)
  local copies, waits for them, and re-layouts  8.93 us (10%)
  other arithmetic  4.08 us (5%)
    pallas_call x1, Pallas kernels, cg_sums(): pl.pallas_call(step_kernel, out_shape=(jax.ShapeDtypeStruct((2, 3, 128, D...  58.5 us
    pallas_call x1, Pallas kernels, circle_weights(): pl.pallas_call(weight_kernel, out_shape=jax.ShapeDtypeStruct((512, 512),...  15.9 us
    unnamed x18, local copies, waits for them, and re-layouts  8.19 us
    add x1, other arithmetic, per_device(): residual_next + ratio[None, None, None, :, None] * (direction * live)  4 us

profile of v1, /device:TPU:1, one launch (start us, length us, event | category | flops | bytes accessed | tf_op | source)
XLA Modules:
  0.0 88.0 jit_solution(16865336010405601624)
XLA Ops:
  0.6 0.7 dynamic_slice.3
  1.4 0.1 compare_convert_fusion
  1.4 0.0 copy-start.2
  1.4 1.0 %copy-done.2 = s32[8,16384]{1,0:T(8,128)S(1)} copy-done((s32[8,16384]{1,0:T(8,128)S(1)}, s32[8,16384]{1,0:T(8,128)}, u32[]{:S(2)}) %copy-start.2) | copy-done | bytes 524312
  2.5 0.0 copy-start.5
  2.5 0.7 copy-done.5
  3.1 15.9 %shard_map.121.g = bf16[512,512]{1,0:T(8,128)(2,1)S(1)} custom-call(s32[32]{0:T(128)S(1)} %copy-done.5, s32[8,16384]{1,0:T(8,128)S(1)} %copy-done.2), custom_call_target="tpu_custom_call" | custom-call | tf_op jit(solution)/shard_map/pallas_call | solution.py:129
  19.0 0.0 copy-start
  19.0 1.9 %copy-done = f32[2,3,2,64,1024]{4,3,2,1,0:T(8,128)S(1)} copy-done((f32[2,3,2,64,1024]{4,3,2,1,0:T(8,128)S(1)}, f32[2,3,2,64,1024]{4,3,2,1,0:T(8,128)}, u32[]{:S(2)}) %copy-start) | copy-done | bytes 3145752
  20.9 0.0 copy-start.1
  20.9 1.9 %copy-done.1 = f32[2,3,2,64,1024]{4,3,2,1,0:T(8,128)S(1)} copy-done((f32[2,3,2,64,1024]{4,3,2,1,0:T(8,128)S(1)}, f32[2,3,2,64,1024]{4,3,2,1,0:T(8,128)}, u32[]{:S(2)}) %copy-start.1) | copy-done | bytes 3145752
  22.8 0.0 copy-start.3
  22.8 0.7 copy-done.3
  23.5 0.0 copy-start.4
  23.5 0.7 copy-done.4
  24.2 0.0 copy-start.6
  24.2 0.7 copy-done.6
  24.9 0.0 copy-start.7
  24.9 0.7 copy-done.7
  25.5 58.5 %shard_map.122 = (f32[2,3,128,1024]{3,2,1,0:T(8,128)S(1)}, f32[8,128]{1,0:T(8,128)S(1)}) custom-call(s32[32]{0:T(128)S(1)} %copy-done.6, f32[2]{0:T(128)S(1)} %copy-done.7, f32[3,1024]{1,0:T(4,128)S(1)} %copy-done.3, f32[1,1024]{1,0:T(1,128)S(1)} %bitcast.11, bf16[512,512]{1,0:T(8,128)(2,1)S(1)} %shard_map.121.g, f32[2,3,128,1024]{3,2,1,0:T(8,128)S(1)} %bitcast.9, ...), custom_call_target="tpu_custom_call" | custom-call | tf_op jit(solution)/shard_map/pallas_call | solution.py:540
  84.0 0.0 copy-start.8
  84.0 4.0 %multiply_add_fusion = (f32[2,3,2,64,1024]{4,3,2,1,0:T(8,128)}, f32[2,3,2,64,1024]{4,3,2,1,0:T(8,128)}) fusion(f32[2,3,2,64,1024]{4,3,2,1,0:T(8,128)S(1)} %copy-done, f32[64]{0:T(128)S(1)} %get-tuple-element.10, f32[2,1024]{1,0:T(2,128)S(1)} %compare_convert_fusion, f32[2,3,2,64,1024]{4,3,2,1,0:T(8,128)S(1)} %bitcast.10, f32[64]{0:T(128)S(1)} %get-tuple-element.9, ...), kind=kLoop, calls=%fused_computation | loop fusion | flops 4718592 | bytes 15737344 | tf_op jit(solution)/shard_map/add | solution.py:625
  88.0 0.0 copy-done.8
  (2 shorter events, 0.0 us)
Async XLA Ops:
  1.4 1.0 %copy-start.2 = (s32[8,16384]{1,0:T(8,128)S(1)}, s32[8,16384]{1,0:T(8,128)}, u32[]{:S(2)}) copy-start(s32[8,16384]{1,0:T(8,128)} %hits.1) | copy-start | bytes 1572868
  2.5 0.7 copy-start.5
  19.0 1.9 %copy-start = (f32[2,3,2,64,1024]{4,3,2,1,0:T(8,128)S(1)}, f32[2,3,2,64,1024]{4,3,2,1,0:T(8,128)}, u32[]{:S(2)}) copy-start(f32[2,3,2,64,1024]{4,3,2,1,0:T(8,128)} %param.11) | copy-start | bytes 9437188
  20.9 1.9 %copy-start.1 = (f32[2,3,2,64,1024]{4,3,2,1,0:T(8,128)S(1)}, f32[2,3,2,64,1024]{4,3,2,1,0:T(8,128)}, u32[]{:S(2)}) copy-start(f32[2,3,2,64,1024]{4,3,2,1,0:T(8,128)} %param.10) | copy-start | bytes 9437188
  22.8 0.7 copy-start.3
  23.5 0.7 copy-start.4
  24.2 0.7 copy-start.6
  24.9 0.7 copy-start.7
  84.0 4.0 %copy-start.8 = (f32[64]{0:T(128)}, f32[64]{0:T(128)S(1)}, u32[]{:S(2)}) copy-start(f32[64]{0:T(128)S(1)} %get-tuple-element.9) | copy-start | bytes 772

commit v2 on v1

v2 whole, which is shorter than its diff:
```python
import functools
import math

import jax
import jax.numpy as jnp
from jax import lax
from jax.experimental import pallas as pl
from jax.experimental.pallas import tpu as pltpu
from jax.sharding import PartitionSpec as P

MESH = pl.DeviceIdType.MESH
BF = jnp.bfloat16
F32 = jnp.float32
NT = (((1,), (1,)), ((), ()))

LAT = 8
ORD = 16
KM = 64
CIRC = 8
NPHI = 16384
LMAX = 8192
LINES = 1024
DEG = LMAX // LAT
CHUNKS = ((0, 1), (1, 2))
AWAY = (2, 1, 3, 0)
SCALE = LMAX / (LINES * NPHI)
LIMIT_MIB = 54


def step_kernel(
    orders_h, noise_h, prior_h, cross_h, hits_h, residual, direction, lz, lp, lm,
    image_out, scal_out,
    orders, noise, prior, cross, hits, res_v, dir_v, lz_v, lp_v, lm_v, ct, cx, cy,
    own, part, prec, summed, relay, fin, phases, rbuf, adj, zbuf, wbuf, img, stat, st1, st2,
    hf, spec, base, gf, g,
    load_sem, out_sem, pair_s, pair_r, ring_s, ring_r, a2a_s, a2a_r, ag_s, ag_r, red_s, red_r,
):
    lat = lax.axis_index("lat")
    ord_ = lax.axis_index("ord")
    x = lat // 2
    core = lat % 2
    partner = 2 * x + (1 - core)
    right = 2 * ((x + 1) % 4) + core
    left = 2 * ((x + 3) % 4) + core
    sent = []

    def remote(src, dst, ssem, rsem, **where):
        copy = pltpu.make_async_remote_copy(
            src_ref=src, dst_ref=dst, send_sem=ssem, recv_sem=rsem,
            device_id=where, device_id_type=MESH,
        )
        copy.start()
        sent.append(copy)
        return copy

    loads = {}

    def load(name, src, dst):
        copy = pltpu.make_async_copy(src, dst, load_sem.at[len(loads)])
        copy.start()
        loads[name] = copy

    def table(name, src, dst, p):
        rows = pl.ds(pl.multiple_of(((x + AWAY[p]) % 4) * 256, 256), 256)
        load((name, p), src.at[:, rows, :], dst.at[:, p])

    load("orders", orders_h, orders)
    load("hits", hits_h, hits)
    load("dir_t", direction.at[:, 0], dir_v.at[:, 0])
    for p in range(4):
        table("z", lz, lz_v, p)
    load("dir_p", direction.at[:, pl.ds(1, 2)], dir_v.at[:, pl.ds(1, 2)])
    for p in range(4):
        table("p", lp, lp_v, p)
        table("m", lm, lm_v, p)
    load("noise", noise_h, noise)
    load("prior", prior_h, prior)
    load("cross", cross_h, cross)
    load("res", residual, res_v)

    barrier = pltpu.get_barrier_semaphore()

    def greet_lat(off, carry):
        pl.semaphore_signal(
            barrier, inc=1, device_id={"lat": (lat + off) % LAT}, device_id_type=MESH
        )
        return carry

    def greet_ord(off, carry):
        pl.semaphore_signal(
            barrier, inc=1, device_id={"ord": (ord_ + off) % ORD}, device_id_type=MESH
        )
        return carry

    lax.fori_loop(1, LAT, greet_lat, 0)
    lax.fori_loop(1, ORD, greet_ord, 0)

    def weight_base():
        lane = lax.broadcasted_iota(jnp.int32, (8, 128), 1)
        parity = lax.broadcasted_iota(jnp.int32, (8, 128), 0) & 1

        def body(m, carry):
            order = orders[m]
            units = (2 * order * lane + order * parity) & (2 * NPHI - 1)
            angle = units.astype(F32) * (math.pi / NPHI)
            size = jnp.where(order == 0, 1.0, 2.0).astype(F32)
            rows = pl.ds(pl.multiple_of(m * 8, 8), 8)
            base[0, rows, :] = size * jnp.cos(angle)
            base[1, rows, :] = -size * jnp.sin(angle)
            return carry

        lax.fori_loop(0, 32, body, 0)

    def weight_spectrum():
        def widen(a, carry):
            hf[pl.ds(pl.multiple_of(a * 8, 8), 8), :] = hits[
                :, pl.ds(pl.multiple_of(a * 128, 128), 128)
            ].astype(F32)
            return carry

        lax.fori_loop(0, 128, widen, 0)
        turns = (
            lax.broadcasted_iota(jnp.int32, (128, 128), 0)
            * lax.broadcasted_iota(jnp.int32, (128, 128), 1)
        ) & 127
        angle = turns.astype(F32) * (2.0 * math.pi / 128)
        wave = jnp.concatenate([jnp.cos(angle), -jnp.sin(angle)], 0)
        high = wave.astype(BF)
        low = (wave - high.astype(F32)).astype(BF)
        wave = jnp.concatenate([high, high, low, low], 1)
        for t in range(CIRC):
            line = hf[pl.ds(t, 128, stride=8), :]
            top = line.astype(BF)
            rest = (line - top.astype(F32)).astype(BF)
            out = jnp.dot(
                wave, jnp.concatenate([top, rest, top, rest], 0), preferred_element_type=F32
            )
            spec[:, t, :] = out

    def weight_rows(lo, hi, blocks):
        lane = lax.broadcasted_iota(jnp.int32, (8, 128), 1)
        diagonal = (lane & 7) == lax.broadcasted_iota(jnp.int32, (8, 128), 0)

        def body(m, carry):
            rows = pl.ds(pl.multiple_of(m * 8, 8), 8)
            re, im = base[0, rows, :], base[1, rows, :]
            order = orders[m]
            for block in range(blocks):
                tiles = [jnp.zeros((8, 128), F32) for _ in range(4)]
                for k in range(16):
                    n = block * 16 + k
                    re2, im2 = base[0, n * 8 : n * 8 + 8, :], base[1, n * 8 : n * 8 + 8, :]
                    up = (order + orders[n]) & 127
                    down = (order - orders[n]) & 127
                    up_re, up_im = spec[up], spec[128 + up]
                    down_re, down_im = spec[down], spec[128 + down]
                    rr, ii, ri, ir = re * re2, im * im2, re * im2, im * re2
                    a_re, a_im = rr - ii, ri + ir
                    b_re, b_im = rr + ii, ir - ri
                    s_re = a_re * up_re - a_im * up_im
                    s_im = a_re * up_im + a_im * up_re
                    d_re = b_re * down_re - b_im * down_im
                    d_im = b_re * down_im + b_im * down_re
                    place = diagonal & (lane // 8 == k)
                    for q, value in enumerate((d_re + s_re, s_im - d_im, s_im + d_im, d_re - s_re)):
                        value = jnp.sum(value, axis=1, keepdims=True)
                        tiles[q] = jnp.where(place, value, tiles[q])
                for q in range(4):
                    gf[q, rows, block * 128 : block * 128 + 128] = 0.5 * tiles[q]
            return carry

        lax.fori_loop(lo, hi, body, 0)

    def weight_matrix():
        for q, mirror in ((0, 0), (1, 2), (2, 1), (3, 3)):
            gf[q, 0:128, 128:256] = gf[mirror, 128:256, 0:128].T
        for s in range(2):
            for u in range(2):
                value = gf[2 * s + (s if u == 0 else 1 - s)]
                top = value.astype(BF)
                rows = slice(s * 256, s * 256 + 256)
                g[rows, u * 256 : u * 256 + 256] = top
                g[rows, 512 + u * 256 : 768 + u * 256] = (value - top.astype(F32)).astype(BF)

    def live_mask(o):
        degree = lax.broadcasted_iota(jnp.int32, (8, DEG), 1) + lat * DEG
        return jnp.where(degree >= orders[2 * ord_ + o], 1.0, 0.0).astype(F32)

    def coefs_t():
        loads["dir_t"].wait()
        for o in range(2):
            mask = jnp.broadcast_to(live_mask(o)[:1], (128, DEG))
            ct[o] = (dir_v[o, 0] * mask).astype(BF)

    def coefs_p():
        loads["dir_p"].wait()
        for o in range(2):
            mask = jnp.broadcast_to(live_mask(o)[:1], (KM, DEG))
            for s in range(2):
                rows = slice(s * KM, (s + 1) * KM)
                e = (dir_v[o, 1, rows, :] * mask).astype(BF)
                b = (dir_v[o, 2, rows, :] * mask).astype(BF)
                cx[o, s * 64 : s * 64 + 64, :] = -e
                cx[o, 128 + s * 64 : 192 + s * 64, :] = -b
                if s == 0:
                    cy[o, 192:256, :] = e
                    cy[o, 64:128, :] = -b
                else:
                    cy[o, 128:192, :] = -e
                    cy[o, 0:64, :] = b

    pairs = {}

    def keep(lo, count, c, first, second):
        both = jnp.concatenate(
            [first.reshape(32 * count, 8, 128), second.reshape(32 * count, 8, 128)], 1
        ).reshape(count, 2, 16, 16, 128)
        own[lo : lo + count, :, c] = both
        part[lo : lo + count, :, c] = both.astype(BF)

    def synth(ch, lo, count):
        c0, nc = CHUNKS[ch]
        cs = pl.ds(c0, nc)
        for p in range(lo, lo + count):
            for name in ("z",) if ch == 0 else ("p", "m"):
                loads[name, p].wait()

        def rows(ref, o):
            return ref[o, lo : lo + count].reshape(count * 256, DEG)

        if ch == 0:
            got = [
                lax.dot_general(rows(lz_v, o), ct[o], NT, preferred_element_type=F32)
                for o in range(2)
            ]
            keep(lo, count, 0, got[0], got[1])
        else:
            got = [
                lax.dot_general(rows(lp_v, o), cx[o], NT, preferred_element_type=F32)
                + lax.dot_general(rows(lm_v, o), cy[o], NT, preferred_element_type=F32)
                for o in range(2)
            ]
            keep(lo, count, 1, got[0][:, :128], got[1][:, :128])
            keep(lo, count, 2, got[0][:, 128:], got[1][:, 128:])
        for p in range(lo, lo + count):
            pairs[ch, p] = remote(
                part.at[p, 1 - core, cs], prec.at[p, cs], pair_s.at[ch, p], pair_r.at[ch, p],
                lat=partner,
            )

    rings = {}
    FAR, RIGHT, LEFT, HERE = range(4)

    def chunk(ch):
        lo, count = CHUNKS[ch]
        return lo, count, pl.ds(lo, count), slice(lo, lo + count)

    def pair_sum(ch, p, lo_g, hi_g):
        _, _, _, c = chunk(ch)
        return own[p, core, c, lo_g:hi_g] + prec[p, c, lo_g:hi_g].astype(F32)

    def ring_far(ch):
        _, _, cs, c = chunk(ch)
        pairs[ch, FAR].wait_recv()
        summed[FAR, c] = pair_sum(ch, FAR, 0, 16).astype(BF)
        a, b = pl.ds(0, 8), pl.ds(8, 8)
        rings[ch, 0] = remote(
            summed.at[FAR, cs, a], relay.at[0, cs], ring_s.at[ch, 0], ring_r.at[ch, 0], lat=right
        )
        rings[ch, 1] = remote(
            summed.at[FAR, cs, b], relay.at[1, cs], ring_s.at[ch, 1], ring_r.at[ch, 1], lat=left
        )

    def ring_near(ch, p, late):
        _, _, cs, c = chunk(ch)
        side = 0 if p == RIGHT else 1
        if late:
            lo_g = 8 * side
            rings[ch, side].wait_recv()
            value = pair_sum(ch, p, lo_g, lo_g + 8) + relay[side, c].astype(F32)
        else:
            lo_g = 8 - 8 * side
            pairs[ch, p].wait_recv()
            value = pair_sum(ch, p, lo_g, lo_g + 8)
        summed[p, c, lo_g : lo_g + 8] = value.astype(BF)
        sem = 2 + side * 2 + late
        span = pl.ds(lo_g, 8)
        rings[ch, sem] = remote(
            summed.at[p, cs, span], fin.at[side, cs, span], ring_s.at[ch, sem], ring_r.at[ch, sem],
            lat=right if p == RIGHT else left,
        )

    def ring_end(ch):
        _, _, _, c = chunk(ch)
        pairs[ch, HERE].wait_recv()
        for sem in (2, 4, 3, 5):
            rings[ch, sem].wait_recv()
        phases[c] = (
            pair_sum(ch, HERE, 0, 16) + fin[0, c].astype(F32) + fin[1, c].astype(F32)
        ).astype(BF)

    drains = []

    def exchange(ch, way, src, dst):
        lo, count, cs, _ = chunk(ch)

        def copy(off):
            to = (ord_ + off) % ORD
            return pltpu.make_async_remote_copy(
                src_ref=src.at[cs, to], dst_ref=dst.at[cs, ord_],
                send_sem=a2a_s.at[way, ch, off], recv_sem=a2a_r.at[way, ch, off],
                device_id={"ord": to}, device_id_type=MESH,
            )

        def go(off, carry):
            copy(off).start()
            return carry

        def wait(off, carry):
            copy(off).wait_recv()
            return carry

        def drain(off, carry):
            copy(off).wait_send()
            return carry

        lax.fori_loop(1, ORD, go, 0)
        for i in range(lo, lo + count):
            dst[i, ord_] = src[i, ord_]
        drains.append(lambda: lax.fori_loop(1, ORD, drain, 0))
        return lambda: lax.fori_loop(1, ORD, wait, 0)

    def apply(ch):
        lo, count, _, _ = chunk(ch)
        left_half = lax.broadcasted_iota(jnp.int32, (256, 128), 1) < KM
        columns = []
        for i in range(lo, lo + count):
            here = rbuf[i].reshape(256, 128)
            swapped = pltpu.roll(here.astype(F32), KM, 1).astype(BF)
            columns.append(jnp.concatenate([here, swapped, here, swapped], 0))
        out = jnp.dot(g[...], jnp.concatenate(columns, 1), preferred_element_type=F32)
        for n, i in enumerate(range(lo, lo + count)):
            lanes = slice(n * 128, n * 128 + 128)
            value = jnp.where(left_half, out[:256, lanes], out[256:, lanes])
            adj[i] = (value * (noise[min(i, 1)] * SCALE)).astype(BF).reshape(16, 16, 128)

    def turn(ch):
        lo, count, _, _ = chunk(ch)
        for i in range(lo, lo + count):
            got = zbuf[i].astype(F32).reshape(16, 2, 8, 128)
            for o in range(2):
                wbuf[lat, i, o] = got[:, o].reshape(128, 128).T.astype(BF)

    gathers = {}

    def gather(ch, i, slot, cs, o, **where):
        view = wbuf.at[slot, cs] if o is None else wbuf.at[slot, cs, o]
        gathers[ch, i] = remote(view, view, ag_s.at[ch, i], ag_r.at[ch, i], **where)

    def gather_start(ch):
        _, _, cs, _ = chunk(ch)
        gather(ch, 1, lat, cs, None, lat=right)
        gather(ch, 2, lat, cs, None, lat=left)
        gather(ch, 0, lat, cs, None, lat=partner)

    def gather_near(ch):
        _, _, cs, _ = chunk(ch)
        gathers[ch, 1].wait_recv()
        gather(ch, 3, left, cs, 0, lat=right)
        gather(ch, 5, left, cs, None, lat=partner)
        gathers[ch, 2].wait_recv()
        gather(ch, 4, right, cs, 1, lat=left)
        gather(ch, 6, right, cs, None, lat=partner)

    def gather_far(ch):
        _, _, cs, _ = chunk(ch)
        far = 2 * ((x + 2) % 4) + core
        gathers[ch, 3].wait_recv()
        gather(ch, 7, far, cs, 0, lat=partner)
        gathers[ch, 4].wait_recv()
        gather(ch, 8, far, cs, 1, lat=partner)

    gather_waits = {HERE: (0,), LEFT: (5,), RIGHT: (6,), FAR: (7, 8)}

    def analysis(ch, lo, count, first):
        quarters = range(lo, lo + count)
        for p in quarters:
            for i in gather_waits[p]:
                gathers[ch, i].wait_recv()
        slots = [2 * ((x + AWAY[p]) % 4) + h for p in quarters for h in range(2)]

        def lines(c, o):
            return jnp.concatenate([wbuf[slot, c, o] for slot in slots], 1)

        def rows(ref, o):
            return ref[o, lo : lo + count].reshape(count * 256, DEG)

        for o in range(2):
            if ch == 0:
                got = jnp.dot(lines(0, o), rows(lz_v, o), preferred_element_type=F32)
                img[o, 0] = got if first else img[o, 0] + got
            else:
                q, u = lines(1, o), lines(2, o)
                straight = jnp.concatenate([-q, -u], 0)
                crossed = jnp.concatenate([u[64:], -u[:64], -q[64:], q[:64]], 0)
                got = jnp.dot(straight, rows(lp_v, o), preferred_element_type=F32) + jnp.dot(
                    crossed, rows(lm_v, o), preferred_element_type=F32
                )
                for c in range(2):
                    piece = got[c * 128 : (c + 1) * 128]
                    img[o, 1 + c] = piece if first else img[o, 1 + c] + piece

    def finish(components, first):
        live = [live_mask(o) for o in range(2)]

        def body(i, carry):
            k0 = pl.multiple_of(i * 8, 8)
            sums = [None] * 4
            for o in range(2):
                for s in range(2):
                    rows = pl.ds(s * KM + k0, 8)
                    search = {}
                    for c in (0, 1) if components == (0,) else (0, 1, 2):
                        search[c] = dir_v[o, c, rows, :] * live[o]
                    for c in components:
                        if c == 0:
                            extra = prior[0:1] * search[0] + cross[...] * search[1]
                        elif c == 1:
                            extra = cross[...] * search[0] + prior[1:2] * search[1]
                        else:
                            extra = prior[2:3] * search[2]
                        image = live[o] * (img[o, c, rows, :] + extra)
                        img[o, c, rows, :] = image
                        current = res_v[o, c, rows, :] * live[o]
                        terms = (
                            current * current, search[c] * image, current * image, image * image,
                        )
                        for q in range(4):
                            part_sum = terms[q][:, :128]
                            for lane in range(128, DEG, 128):
                                part_sum = part_sum + terms[q][:, lane : lane + 128]
                            sums[q] = part_sum if sums[q] is None else sums[q] + part_sum
            for q in range(4):
                rows = pl.ds(k0, 8)
                stat[q, rows, :] = sums[q] if first else stat[q, rows, :] + sums[q]
            return carry

        lax.fori_loop(0, KM // 8, body, 0)

    stores = []

    def store(c0, nc):
        copy = pltpu.make_async_copy(
            img.at[:, pl.ds(c0, nc)], image_out.at[:, pl.ds(c0, nc)], out_sem.at[len(stores)]
        )
        copy.start()
        stores.append(copy)

    def all_reduce(buf, axis, size, me, stage):
        def copy(off):
            return pltpu.make_async_remote_copy(
                src_ref=buf.at[me], dst_ref=buf.at[me],
                send_sem=red_s.at[stage, off], recv_sem=red_r.at[stage, off],
                device_id={axis: (me + off) % size}, device_id_type=MESH,
            )

        def go(off, carry):
            copy(off).start()
            return carry

        def wait(off, carry):
            copy(off).wait_recv()
            return carry

        def drain(off, carry):
            copy(off).wait_send()
            return carry

        lax.fori_loop(1, size, go, 0)
        drains.append(lambda: lax.fori_loop(1, size, drain, 0))
        lax.fori_loop(1, size, wait, 0)
        total = buf[0]
        for i in range(1, size):
            total = total + buf[i]
        return total

    loads["orders"].wait()
    weight_base()
    loads["hits"].wait()
    weight_spectrum()
    coefs_t()
    pl.semaphore_wait(barrier, LAT + ORD - 2)
    synth(0, 0, 4)
    coefs_p()
    ring_far(0)
    ring_near(0, RIGHT, 0)
    ring_near(0, LEFT, 0)
    synth(1, 0, 2)
    ring_near(0, RIGHT, 1)
    ring_near(0, LEFT, 1)
    synth(1, 2, 2)
    ring_far(1)
    ring_near(1, RIGHT, 0)
    ring_near(1, LEFT, 0)
    ring_end(0)
    wait_a = exchange(0, 0, phases, rbuf)
    weight_rows(0, 16, 1)
    ring_near(1, RIGHT, 1)
    ring_near(1, LEFT, 1)
    weight_rows(16, 32, 2)
    weight_matrix()
    loads["noise"].wait()
    wait_a()
    apply(0)
    wait_b = exchange(0, 1, adj, zbuf)
    ring_end(1)
    wait_c = exchange(1, 0, phases, rbuf)
    wait_b()
    turn(0)
    gather_start(0)
    wait_c()
    apply(1)
    wait_d = exchange(1, 1, adj, zbuf)
    gather_near(0)
    analysis(0, HERE, 1, True)
    wait_d()
    turn(1)
    gather_start(1)
    gather_far(0)
    analysis(0, RIGHT, 2, False)
    analysis(0, FAR, 1, False)
    gather_near(1)
    for name in ("prior", "cross", "res"):
        loads[name].wait()
    finish((0,), True)
    store(0, 1)
    analysis(1, HERE, 1, True)
    gather_far(1)
    analysis(1, RIGHT, 2, False)
    analysis(1, FAR, 1, False)
    finish((1, 2), False)
    store(1, 2)

    column = lax.broadcasted_iota(jnp.int32, (KM, 128), 1)
    tile = jnp.zeros((KM, 128), F32)
    for q in range(4):
        tile = jnp.where(column == q, jnp.sum(stat[q], axis=1, keepdims=True), tile)
    st1[lat] = jnp.concatenate([tile, tile], 0).T[:8]
    st2[ord_] = all_reduce(st1, "lat", LAT, lat, 0)
    total = all_reduce(st2, "ord", ORD, ord_, 1)
    norm_now, curvature, mixed, square = (total[q : q + 1] for q in range(4))
    step_size = norm_now / curvature
    norm_next = norm_now + step_size * (step_size * square - 2.0 * mixed)
    ratio = norm_next / norm_now
    sub = lax.broadcasted_iota(jnp.int32, (8, 128), 0)
    rows = jnp.where(sub == 0, step_size, ratio)
    for o in range(2):
        start = (orders[2 * ord_ + o] - lat * DEG).astype(F32)
        rows = jnp.where(sub == 2 + o, start, rows)
    scal_out[...] = rows

    for drain in drains:
        drain()
    for copy in sent:
        copy.wait_send()
    for copy in stores:
        copy.wait()


def cg_sums(*operands):
    vmem = pl.BlockSpec(memory_space=pltpu.VMEM)
    hbm = pl.BlockSpec(memory_space=pltpu.HBM)
    dma = pltpu.SemaphoreType.DMA
    nch = len(CHUNKS)
    return pl.pallas_call(
        step_kernel,
        out_shape=(
            jax.ShapeDtypeStruct((2, 3, 128, DEG), F32),
            jax.ShapeDtypeStruct((8, 128), F32),
        ),
        in_specs=[hbm] * 10,
        out_specs=(pl.BlockSpec(memory_space=pl.ANY), vmem),
        scratch_shapes=[
            pltpu.SMEM((32,), jnp.int32),
            pltpu.SMEM((2,), F32),
            pltpu.VMEM((3, DEG), F32),
            pltpu.VMEM((1, DEG), F32),
            pltpu.VMEM((CIRC, NPHI), jnp.int32),
            pltpu.VMEM((2, 3, 128, DEG), F32),
            pltpu.VMEM((2, 3, 128, DEG), F32),
            pltpu.VMEM((2, 4, 256, DEG), BF),
            pltpu.VMEM((2, 4, 256, DEG), BF),
            pltpu.VMEM((2, 4, 256, DEG), BF),
            pltpu.VMEM((2, 128, DEG), BF),
            pltpu.VMEM((2, 256, DEG), BF),
            pltpu.VMEM((2, 256, DEG), BF),
            pltpu.VMEM((4, 2, 3, 16, 16, 128), F32),
            pltpu.VMEM((4, 2, 3, 16, 16, 128), BF),
            pltpu.VMEM((4, 3, 16, 16, 128), BF),
            pltpu.VMEM((4, 3, 16, 16, 128), BF),
            pltpu.VMEM((2, 3, 8, 16, 128), BF),
            pltpu.VMEM((2, 3, 16, 16, 128), BF),
            pltpu.VMEM((3, 16, 16, 128), BF),
            pltpu.VMEM((3, 16, 16, 128), BF),
            pltpu.VMEM((3, 16, 16, 128), BF),
            pltpu.VMEM((3, 16, 16, 128), BF),
            pltpu.VMEM((LAT, 3, 2, 128, 128), BF),
            pltpu.VMEM((2, 3, 128, DEG), F32),
            pltpu.VMEM((4, KM, 128), F32),
            pltpu.VMEM((LAT, 8, 128), F32),
            pltpu.VMEM((ORD, 8, 128), F32),
            pltpu.VMEM((128 * CIRC, 128), F32),
            pltpu.VMEM((256, CIRC, 128), F32),
            pltpu.VMEM((2, 256, 128), F32),
            pltpu.VMEM((4, 256, 256), F32),
            pltpu.VMEM((512, 1024), BF),
            dma((20,)),
            dma((2,)),
            dma((nch, 4)),
            dma((nch, 4)),
            dma((nch, 6)),
            dma((nch, 6)),
            dma((2, nch, ORD)),
            dma((2, nch, ORD)),
            dma((nch, 9)),
            dma((nch, 9)),
            dma((2, ORD)),
            dma((2, ORD)),
        ],
        compiler_params=pltpu.CompilerParams(
            collective_id=0, has_side_effects=True, vmem_limit_bytes=LIMIT_MIB * 2**20
        ),
    )(*operands)


def per_device(
    residual,
    direction,
    legendre_zero,
    legendre_plus,
    legendre_minus,
    order_pairs,
    hit_counts,
    noise_weight,
    prior_inverse,
    prior_cross,
):
    shape = residual.shape
    flat = (2, 3, 128, DEG)
    image, scalars = cg_sums(
        order_pairs,
        noise_weight,
        prior_inverse,
        prior_cross.reshape(1, DEG),
        hit_counts,
        residual.reshape(flat),
        direction.reshape(flat),
        legendre_zero,
        legendre_plus,
        legendre_minus,
    )
    step_size = scalars[0, :KM]
    ratio = scalars[1, :KM]
    start = scalars[2:4, 0]
    live = (jnp.arange(DEG, dtype=F32)[None, :] >= start[:, None]).astype(F32)
    live = live[:, None, None, None, :]
    residual_next = (
        residual * live - step_size[None, None, None, :, None] * image.reshape(shape)
    )
    direction_next = residual_next + ratio[None, None, None, :, None] * (direction * live)
    return residual_next, direction_next, step_size


def solution(mesh):
    coef = P("ord", None, None, None, "lat")
    table = P("ord", None, "lat")
    in_specs = (
        coef, coef, table, table, table, P(), P(("lat", "ord"), None), P(), P(None, "lat"), P("lat"),
    )
    return jax.shard_map(
        per_device, mesh=mesh, in_specs=in_specs, out_specs=(coef, coef, P()), check_vma=False
    )
```

time: 88.4 us -> 69.7 us (0.79)
  Pallas kernels: 74.3 us -> 60.6 us
  local copies, waits for them, and re-layouts: 8.93 us -> 1.57 us
  other arithmetic: 4.08 us -> 6.58 us
    pallas_call x1 -> x0, Pallas kernels: 15.9 us -> none  [circle_weights(): pl.pallas_call(weight_kernel, out_shape=jax.ShapeDtypeStruct((512, 512),...]
    unnamed x18 -> x6, local copies, waits for them, and re-layouts: 8.19 us -> 0.01 us
    add x1, other arithmetic: 4 us -> 6.51 us  [per_device(): residual_next + ratio[None, None, None, :, None] * (direction * live)]
    pallas_call x1, Pallas kernels: 58.5 us -> 60.6 us  [cg_sums(): pl.pallas_call(step_kernel, out_shape=(jax.ShapeDtypeStruct((2, 3, 128, D...]
where the time goes in v2:
time: 69.7 us; the launch traced here: 69.4 us
  Pallas kernels  60.6 us (87%)
  other arithmetic  6.58 us (9%)
  local copies, waits for them, and re-layouts  1.57 us (2%)
    pallas_call x1, Pallas kernels, cg_sums(): pl.pallas_call(step_kernel, out_shape=(jax.ShapeDtypeStruct((2, 3, 128, D...  60.6 us
    add x1, other arithmetic, per_device(): residual_next + ratio[None, None, None, :, None] * (direction * live)  6.51 us

profile of v2, /device:TPU:1, one launch (start us, length us, event | category | flops | bytes accessed | tf_op | source)
XLA Modules:
  0.0 69.4 jit_solution(3081825176705980534)
XLA Ops:
  0.6 0.0 copy-start
  0.6 0.0 copy-start.1
  0.7 60.6 %shard_map.121 = (f32[2,3,128,1024]{3,2,1,0:T(8,128)}, f32[8,128]{1,0:T(8,128)}) custom-call(s32[32]{0:T(128)} %orders_h.1, f32[2]{0:T(128)} %noise_h.1, f32[3,1024]{1,0:T(4,128)} %prior_h.1, f32[1,1024]{1,0:T(1,128)} %bitcast.11, s32[8,16384]{1,0:T(8,128)} %hits_h.1, f32[2,3,128,1024]{3,2,1,0:T(8,128)} %bitcast.9, f32[2,3,128,1024]{3,2,1,0:T(8,128)} %bitcast.8, ...), custom_call_target="tpu_custom_call" | custom-call | tf_op jit(solution)/shard_map/pallas_call | solution.py:575
  61.3 0.8 %slice_reduce_fusion = f32[2]{0:T(128)S(1)} fusion(f32[8,128]{1,0:T(8,128)} %get-tuple-element.5), kind=kLoop, calls=%fused_computation.3 | loop fusion | bytes 16 | tf_op jit(solution)/shard_map/slice | solution.py:664
  62.1 0.8 %slice_bitcast_fusion.1 = (f32[64]{0:T(128)S(1)}, f32[64]{0:T(128)S(1)}) fusion(f32[8,128]{1,0:T(8,128)} %get-tuple-element.5), kind=kLoop, calls=%fused_computation.5 | loop fusion | bytes 1024 | tf_op jit(solution)/shard_map/mul | solution.py:668
  62.9 0.0 copy-start.2
  62.9 0.1 compare_convert_fusion
  62.9 0.0 copy-done
  62.9 0.0 copy-done.1
  62.9 6.5 %multiply_add_fusion = (f32[2,3,2,64,1024]{4,3,2,1,0:T(8,128)}, f32[2,3,2,64,1024]{4,3,2,1,0:T(8,128)}) fusion(f32[2,3,2,64,1024]{4,3,2,1,0:T(8,128)S(1)} %copy-done, f32[64]{0:T(128)S(1)} %get-tuple-element.10, f32[2,1024]{1,0:T(2,128)S(1)} %compare_convert_fusion, f32[2,3,2,64,1024]{4,3,2,1,0:T(8,128)} %bitcast.10, f32[64]{0:T(128)S(1)} %get-tuple-element.9, ...), kind=kLoop, calls=%fused_computation | loop fusion | flops 4718592 | bytes 15737344 | tf_op jit(solution)/shard_map/add | solution.py:670
  69.4 0.0 copy-done.2
Async XLA Ops:
  0.6 62.3 %copy-start = (f32[2,3,2,64,1024]{4,3,2,1,0:T(8,128)S(1)}, f32[2,3,2,64,1024]{4,3,2,1,0:T(8,128)}, u32[]{:S(2)}) copy-start(f32[2,3,2,64,1024]{4,3,2,1,0:T(8,128)} %param.11) | copy-start | bytes 9437188
  0.6 62.3 %copy-start.1 = (f32[2,3,2,64,1024]{4,3,2,1,0:T(8,128)S(1)}, f32[2,3,2,64,1024]{4,3,2,1,0:T(8,128)}, u32[]{:S(2)}) copy-start(f32[2,3,2,64,1024]{4,3,2,1,0:T(8,128)} %param.10) | copy-start | bytes 9437188
  62.9 6.6 %copy-start.2 = (f32[64]{0:T(128)}, f32[64]{0:T(128)S(1)}, u32[]{:S(2)}) copy-start(f32[64]{0:T(128)S(1)} %get-tuple-element.9) | copy-start | bytes 772
